TPU v7x, 1024 devices: a whole 4x4x32 slice. The times are simulated.
1024 devices in a mesh: row: 64 (over z, core), col: 16 (over x, y).
Axes of the slice: x: 4, y: 4, z: 32, core: 2. Of those that a mesh axis runs over, the one named last changes fastest.
Arguments:
- block_values: float32 [16384, 8192], P('col', 'row'), may hold values from -4 to 4
- block_cols: int32 [128, 64], P('col', 'row'), may hold values from 0 to 1, as said below
- section_cols: int32 [2], replicated, may hold values from 0 to 63
Outputs:
- updated: bfloat16 [16384, 8192], P('col', 'row')
Inputs may be any that keep to these rules, and one draw needn't show every extreme that they name: `block_cols`: within each block row, the 1 entries belonging to one index of row are distinct.
All inputs are finite; a program needn't handle non-finite values.
Results may differ from a plain program's by a relative error of at most 0.001.
Values sent between devices are 32-bit elements; how exact they have to be, the bound alone decides.
A program may use at most 32 MiB of HBM per device.

v0:
```python
import jax
import jax.numpy as jnp
from jax import lax
from jax.sharding import PartitionSpec as P

CB = 2
SECTIONS = 2


def from_root(x, axis, root):
    mine = lax.axis_index(axis) == root
    return lax.psum(jnp.where(mine, x, jnp.zeros_like(x)), axis)


def contribution(panel_values, panel_cols, band_values, band_cols, own_cols):
    picked = band_values[panel_cols]
    picked_cols = band_cols[panel_cols]
    matches = (picked_cols[:, :, None, :] == own_cols[:, None, :, None]).astype(jnp.float32)
    selected = jnp.einsum("ipgq,ipyqz->ipgyz", matches, picked, precision=lax.Precision.HIGHEST)
    return jnp.einsum("ixpy,ipgyz->ixgz", panel_values, selected, precision=lax.Precision.HIGHEST)


def shards(block_values, block_cols, section_cols):
    tile_rows = block_cols.shape[0]
    slot_count = block_cols.shape[1]
    block_size = block_values.shape[1] // slot_count
    own_values = block_values.reshape(tile_rows, block_size, slot_count, block_size)
    total = jnp.zeros((tile_rows, block_size, slot_count, block_size), jnp.float32)
    for section_index in range(SECTIONS):
        first_group = section_cols[section_index]
        panel_values, panel_cols = (
            from_root(block_values, "row", first_group),
            from_root(block_cols, "row", first_group),
        )
        first_row = first_group * CB
        band_owner = first_row // tile_rows
        band_start = first_row % tile_rows
        whole_values, whole_cols = (
            from_root(block_values, "col", band_owner),
            from_root(block_cols, "col", band_owner),
        )
        band_values = lax.dynamic_slice_in_dim(
            whole_values, band_start * block_size, CB * block_size, 0
        )
        band_cols = lax.dynamic_slice_in_dim(whole_cols, band_start, CB, 0)
        total = total + contribution(
            panel_values.reshape(tile_rows, block_size, slot_count, block_size),
            panel_cols,
            band_values.reshape(CB, block_size, slot_count, block_size),
            band_cols,
            block_cols,
        )
    updated = 1.5 * own_values - 0.5 * total - 0.1 * total * total * total
    return updated.astype(jnp.bfloat16).reshape(tile_rows * block_size, slot_count * block_size)


def solution(mesh):
    return jax.shard_map(
        shards,
        mesh=mesh,
        in_specs=(P("col", "row"), P("col", "row"), P()),
        out_specs=P("col", "row"),
        check_vma=False,
    )
```

profile of v0, /device:TPU:1, one launch (start us, length us, event | category | flops | bytes accessed | tf_op | source)
XLA Modules:
  0.0 600.9 jit_solution(6336095154261263649)
XLA Ops:
  6.5 0.0 all-reduce.9.cloned.1.call-start
  6.5 1.3 fusion.11
  10.5 2.4 broadcast_select_fusion
  12.9 0.0 all-reduce.9.cloned.1.call-update
  12.9 0.0 all-reduce.7.cloned.1.call-start
  13.0 0.7 all-reduce.7.cloned.1.call-update
  13.7 0.0 copy-start.1
  13.7 0.6 copy-done.1
  14.4 42.6 %all-reduce = (s32[8,1]{0,1:T(1,128)S(1)}, s32[8,1]{0,1:T(1,128)S(1)}) all-reduce(s32[8,1]{0,1:T(1,128)S(1)} %get-tuple-element.21, s32[8,1]{0,1:T(1,128)S(1)} %get-tuple-element.23), channel_id=1, replica_groups=mesh['row'=64,'col'=16] {'row'}, use_global_device_ids=true, to_apply=%region_2.3 | all-reduce | flops 16 | bytes 128 | tf_op jit(solution)/shard_map/psum | solution.py:12
  57.1 13.0 %all-reduce.1 = (s32[8,1]{0,1:T(1,128)S(1)}, s32[8,1]{0,1:T(1,128)S(1)}) all-reduce(s32[8,1]{0,1:T(1,128)S(1)} %get-tuple-element.22, s32[8,1]{0,1:T(1,128)S(1)} %get-tuple-element.20), channel_id=1, replica_groups=mesh['row'=64,'col'=16] {'col'}, use_global_device_ids=true, to_apply=%region_1.2 | all-reduce | flops 16 | bytes 128 | tf_op jit(solution)/shard_map/psum | solution.py:12
  70.1 0.1 fusion.7
  70.1 0.6 gather_fusion
  70.8 0.6 gather_fusion.2
  71.5 107.6 %all-reduce.9.cloned.1.call-done = (f32[1024,128]{1,0:T(8,128)}, f32[1024,128]{1,0:T(8,128)}) async-done(((f32[1024,128]{1,0:T(8,128)}, f32[1024,128]{1,0:T(8,128)}), (f32[1024,128]{1,0:T(8,128)}, f32[1024,128]{1,0:T(8,128)})) %all-reduce.9.cloned.1.call-update) | async-done | bytes 1048592 | tf_op jit(solution)/shard_map/psum | solution.py:12
  179.0 1.0 constant_dynamic-slice_fusion
  180.0 0.6 gather_fusion.1
  180.6 0.6 gather_fusion.3
  181.2 409.6 %all-reduce.7.cloned.1.call-done = (f32[8,128,128]{2,1,0:T(8,128)}, f32[8,128,128]{2,1,0:T(8,128)}) async-done(((f32[8,128,128]{2,1,0:T(8,128)}, f32[8,128,128]{2,1,0:T(8,128)}), (f32[8,128,128]{2,1,0:T(8,128)}, f32[8,128,128]{2,1,0:T(8,128)})) %all-reduce.7.cloned.1.call-update) | async-done | bytes 1048592 | tf_op jit(solution)/shard_map/psum | solution.py:12
  590.8 0.0 copy-start
  590.8 1.8 fusion.3
  592.6 0.0 copy-done
  592.6 1.5 fusion.1
  (5 shorter events, 0.0 us)
Async XLA Ops:
  6.5 172.5 %all-reduce.9.cloned.1.call-start = ((), (), s32[]{:S(2)}) async-start(), calls=%async_computation.1 | async-start | bytes 2097152 | tf_op jit(solution)/shard_map/psum | solution.py:12
  12.9 577.8 %all-reduce.7.cloned.1.call-start = ((), (), s32[]{:S(2)}) async-start(), calls=%async_computation | async-start | bytes 2097152 | tf_op jit(solution)/shard_map/psum | solution.py:12
  13.7 0.7 copy-start.1
  590.8 1.8 copy-start
Sparse Core Ops, SparseCore 0:
  13.0 165.9 all-reduce.8
  181.4 409.3 all-reduce.6
where the time goes:
time: 601 us
  waiting for transfers between devices  518 us (86%)
  blocking collectives  55.7 us (9%)
  between operations  16.1 us (3%)
    psum x2, waiting for transfers between devices, from_root(): return lax.psum(jnp.where(mine, x, jnp.zeros_like(x)), axis)  517 us
    psum x2, blocking collectives, from_root(): return lax.psum(jnp.where(mine, x, jnp.zeros_like(x)), axis)  55.7 us
  transfers between devices with their start and end apart: 2, of which 2 were waited for; matrix products, arithmetic and copies ran while one was open for 1% of the time, Pallas kernels for 0%

commit v1 on v0

v1 whole, which is shorter than its diff:
```python
import functools

import jax
import jax.numpy as jnp
from jax import lax
from jax.experimental import pallas as pl
from jax.experimental.pallas import tpu as pltpu
from jax.sharding import PartitionSpec as P

MESH = pl.DeviceIdType.MESH
BLK = 128
TILE = 8
UNITS = 8
STRIDE = 4
GROUPS = 3
PER = 3
CHUNKS = GROUPS * PER
LANES = 5
SIDE = 4


def broadcast_multiply(
    n_row, sec_ref, cols_ref, x_hbm, o_ref,
    xv, xs, raw, rawh, cand, tx, rx, pan, sib, stage, bx, by, bnd, wh, wl,
    x_sem, rs_s, rs_r, rh_s, rh_r, cv_s, cv_r, ag_s, ag_r, ah_s, ah_r, sb_s, sb_r, bs_s, bs_r,
):
    chips = n_row // 2
    blocks = chips // STRIDE
    hops = (blocks // 2, (blocks - 1) // 2)
    slots = tuple(CHUNKS + LANES * (d - 1) for d in hops)
    row = lax.axis_index("row")
    col = lax.axis_index("col")
    z, core = lax.div(row, 2), lax.rem(row, 2)
    cx, cy = lax.div(col, SIDE), lax.rem(col, SIDE)

    def at(dz, k):
        return lax.rem(z + dz + chips, chips) * 2 + k

    def unit(r):
        return lax.rem(r, UNITS)

    sibling = at(0, 1 - core)
    near = [at(dz, k) for dz in (-1, 1) for k in (0, 1)]
    far = [at(dz, k) for dz in (-2, 2) for k in (0, 1)]
    xs_peers = [lax.rem(cx + d, SIDE) for d in range(1, SIDE)]
    ys_peers = [lax.rem(cy + d, SIDE) for d in range(1, SIDE)]

    barrier = pltpu.get_barrier_semaphore()
    greet = [(r, col) for r in near + far + [sibling]]
    greet += [(row, px * SIDE + cy) for px in xs_peers]
    greet += [(row, cx * SIDE + py) for py in ys_peers]
    for device in greet:
        pl.semaphore_signal(barrier, inc=1, device_id=device, device_id_type=MESH)

    load = pltpu.make_async_copy(x_hbm, xv, x_sem)
    load.start()
    load.wait()

    sent = []

    def send(src, dst, send_sem, recv_sem, device):
        copy = pltpu.make_async_remote_copy(
            src_ref=src, dst_ref=dst, send_sem=send_sem, recv_sem=recv_sem,
            device_id=device, device_id_type=MESH,
        )
        copy.start()
        sent.append(copy)
        return copy

    for u in range(UNITS):
        mark = jnp.full((TILE, BLK), cols_ref[u, 0].astype(jnp.float32), jnp.float32)
        for h in range(2):
            xs[u, 0, h, 0] = mark
            for k in range(1, CHUNKS):
                first = u * BLK + h * (BLK // 2) + (k - 1) * TILE
                xs[u, k // PER, h, k % PER] = xv[first : first + TILE, :]
    groups = [jnp.full((TILE, BLK), sec_ref[s], jnp.int32) for s in range(2)]
    for s in range(2):
        for q in range(2):
            for first in range(0, BLK + TILE, TILE):
                value = None
                for i in range(UNITS // 2):
                    u = 2 * i + q
                    if first == 0:
                        piece = jnp.full((TILE, BLK), cols_ref[u, 0].astype(jnp.float32), jnp.float32)
                    else:
                        start = u * BLK + first - TILE
                        piece = xv[start : start + TILE, :]
                    value = piece if i == 0 else jnp.where((groups[s] & 3) == i, piece, value)
                stage[2 * s + q, first : first + TILE] = value

    pl.semaphore_wait(barrier, len(greet))

    full_copies, half_copies = [], []
    for g in range(GROUPS):
        line = []
        for dz in (1, -1):
            for k in (0, 1):
                r = at(dz, k)
                slot = (1 if dz == 1 else 3) + core
                i = (0 if dz == 1 else 2) + k
                line.append(send(
                    xs.at[unit(r), g], raw.at[slot, g], rs_s.at[i, g], rs_r.at[slot, g], (r, col)
                ))
        line.append(send(
            xs.at[unit(sibling), g], raw.at[0, g], rs_s.at[4, g], rs_r.at[0, g], (sibling, col)
        ))
        full_copies.append(line)
        for dz in (2, -2):
            for k in (0, 1):
                r = at(dz, k)
                h = 0 if dz == 2 else 1
                slot = 2 * h + core
                i = 2 * h + k
                half_copies.append(send(
                    xs.at[unit(r), g, h], rawh.at[slot, g], rh_s.at[i, g], rh_r.at[slot, g], (r, col)
                ))

    def spread(src, dst, mine, peers, device, step):
        for d, p in enumerate(peers):
            send(src(p), dst.at[mine], bs_s.at[step, d], bs_r.at[step, mine], device(p))

    def arrived(dst, peers, step):
        for p in peers:
            pltpu.make_async_copy(dst.at[p], dst.at[p], bs_r.at[step, p]).wait()

    spread(lambda p: stage.at[p], bx, cx, xs_peers, lambda p: (row, p * SIDE + cy), 0)

    where_right = []
    for h in range(2):
        line = []
        for s in range(2):
            e = (z - (groups[s] >> 1)) & (chips - 1)
            m = e & (STRIDE - 1)
            v = jnp.where(m == 2, 2 if h == 0 else -2, jnp.where(m == 3, -1, m))
            line.append(((e - v) & (chips - 1)) >> 2)
        where_right.append(line)

    def wait_for(dst, sem):
        pltpu.make_async_copy(dst, dst, sem).wait()

    me_unit = unit(row)
    sources = [sibling] + near
    right4 = (at(STRIDE, core), col)
    left4 = (at(-STRIDE, core), col)

    def candidate(k):
        g, c = k // PER, k % PER
        for h in range(2):
            own = xs[me_unit, g, h, c]
            pieces = [(sources[i], raw[i, g, h, c]) for i in range(5)]
            pieces += [(far[2 * h + i], rawh[2 * h + i, g, c]) for i in range(2)]
            for s in range(2):
                value = own
                for r, piece in pieces:
                    value = jnp.where(groups[s] == r, piece, value)
                cand[k, h, s] = value
                pan[0, g, h, s, c] = value

    def consume(d, t):
        for hop in range(1, hops[d] + 1):
            k = t - LANES * (hop - 1)
            if 0 <= k < CHUNKS:
                g, c = k // PER, k % PER
                place = hop if d == 0 else blocks - hop
                for h in range(2):
                    for s in range(2):
                        pan[0, g, h, s, c] = jnp.where(
                            where_right[h][s] == place, rx[d, t, h, s], pan[0, g, h, s, c]
                        )

    def gather(g):
        send(pan.at[0, g], pan.at[1, g], ag_s.at[0, g], ag_r.at[0, g], (at(1, core), col))
        send(pan.at[0, g], pan.at[2, g], ag_s.at[1, g], ag_r.at[1, g], (at(-1, core), col))
        send(pan.at[0, g, 0], pan.at[3, g, 0], ah_s.at[0, g], ah_r.at[0, g], (at(2, core), col))
        send(pan.at[0, g, 1], pan.at[3, g, 1], ah_s.at[1, g], ah_r.at[1, g], (at(-2, core), col))
        send(pan.at[0, g], sib.at[0, g], sb_s.at[0, g], sb_r.at[0, g], (sibling, col))

    def pick(dst, into, mine, own, peers, place):
        for first in range(0, BLK + TILE, TILE):
            rows = pl.ds(first, TILE)
            value = own(rows)
            for p in peers:
                value = jnp.where(place == p, dst[p, rows], value)
            into[mine, rows] = value

    my_group = jnp.full((TILE, BLK), sec_ref[lax.div(cx, 2)], jnp.int32)

    def band_step_two():
        arrived(bx, xs_peers, 0)
        pick(bx, by, cy, lambda rows: stage[cx, rows], xs_peers, my_group >> 4)
        spread(lambda p: by.at[cy], by, cy, ys_peers, lambda p: (row, cx * SIDE + p), 1)

    def band_step_three():
        arrived(by, ys_peers, 1)
        pick(by, bnd, cx, lambda rows: by[cy, rows], ys_peers, (my_group >> 2) & 3)
        spread(lambda p: bnd.at[cx], bnd, cx, xs_peers, lambda p: (row, p * SIDE + cy), 2)

    def band_ready():
        arrived(bnd, xs_peers, 2)
        for s in range(2):
            for q in range(2):
                value = bnd[2 * s + q, TILE:]
                high = value.astype(jnp.bfloat16)
                low = (value - high.astype(jnp.float32)).astype(jnp.bfloat16)
                wh[s, :BLK, q * BLK : (q + 1) * BLK] = high
                wh[s, BLK:, q * BLK : (q + 1) * BLK] = high
                wl[s, :, q * BLK : (q + 1) * BLK] = low

    def received(d, t):
        wait_for(rx.at[d, t], cv_r.at[d, t])

    def finish(t):
        k = t - LANES * (hops[0] - 1)
        if k >= 0 and k % PER == PER - 1:
            gather(k // PER)

    for t in range(slots[0]):
        if t < CHUNKS and t % PER == 0:
            g = t // PER
            for i in range(5):
                wait_for(raw.at[i, g], rs_r.at[i, g])
            for i in range(4):
                wait_for(rawh.at[i, g], rh_r.at[i, g])
            for k in range(t, t + PER):
                candidate(k)
        for d in range(2):
            if t >= slots[d]:
                continue
            target = right4 if d == 0 else left4
            if t >= LANES:
                received(d, t - LANES)
            if t < CHUNKS:
                for h in range(2):
                    for s in range(2):
                        value = cand[t, h, s]
                        if t >= LANES:
                            value = jnp.where(where_right[h][s] == 0, value, rx[d, t - LANES, h, s])
                        tx[d, t, h, s] = value
                source = tx.at[d, t]
            else:
                source = rx.at[d, t - LANES]
            send(source, rx.at[d, t], cv_s.at[d, t], cv_r.at[d, t], target)
        if t >= LANES:
            for d in range(2):
                if t < slots[d]:
                    consume(d, t - LANES)
            if t >= slots[1] and t - LANES < slots[1]:
                received(1, t - LANES)
                consume(1, t - LANES)
            finish(t - LANES)
        if t == LANES - 1:
            band_step_two()
        if t == 2 * LANES - 1:
            band_step_three()
        if t == 3 * LANES - 1:
            band_ready()
    for t in range(slots[0] - LANES, slots[0]):
        if t < slots[1]:
            received(1, t)
            consume(1, t)
        received(0, t)
        consume(0, t)
        finish(t)

    def multiply(buf, i, u):
        total = jnp.zeros((BLK, BLK), jnp.float32)
        own_col = cols_ref[u, 0].astype(jnp.float32)
        for s in range(2):
            tiles = [
                buf[i, k // PER, h, s, k % PER] for h in range(2) for k in range(1, CHUNKS)
            ]
            value = jnp.concatenate(tiles, axis=0)
            high = value.astype(jnp.bfloat16)
            low = (value - high.astype(jnp.float32)).astype(jnp.bfloat16)
            both = jnp.concatenate([high, low], axis=1)
            product = jnp.dot(both, wh[s], preferred_element_type=jnp.float32)
            product += jnp.dot(high, wl[s], preferred_element_type=jnp.float32)
            second = buf[i, 0, 0, s, 0][0:1, :] > 0.5
            mark = jnp.where(second, bnd[2 * s + 1, 0:1, :], bnd[2 * s, 0:1, :])
            part = jnp.where(second, product[:, BLK:], product[:, :BLK])
            total += jnp.where(mark == own_col, part, 0.0)
        rows = pl.ds(pl.multiple_of(u * BLK, BLK), BLK)
        own = xv[rows, :]
        o_ref[rows, :] = (1.5 * own - 0.5 * total - 0.1 * total * total * total).astype(jnp.bfloat16)

    steps = (0, -2, 2, 4)

    def unit_at(r, i):
        return lax.rem(r + steps[i] + UNITS, UNITS)

    for i in (1, 2, 3):
        for g in range(GROUPS):
            if i < 3:
                wait_for(pan.at[i, g], ag_r.at[i - 1, g])
            else:
                wait_for(pan.at[3, g, 0], ah_r.at[0, g])
                wait_for(pan.at[3, g, 1], ah_r.at[1, g])
            send(pan.at[i, g], sib.at[i, g], sb_s.at[i, g], sb_r.at[i, g], (sibling, col))
    for i in range(4):
        multiply(pan, i, unit_at(row, i))
    for i in range(4):
        for g in range(GROUPS):
            wait_for(sib.at[i, g], sb_r.at[i, g])
        multiply(sib, i, unit_at(sibling, i))
    for copy in sent:
        copy.wait_send()


def shards(n_row, block_values, block_cols, section_cols):
    blocks = n_row // 2 // STRIDE
    slots = CHUNKS + LANES * (blocks // 2 - 1)
    f32 = jnp.float32
    part = (2, PER, TILE, BLK)
    packet = (2, 2, TILE, BLK)
    held = (GROUPS, 2, 2, PER, TILE, BLK)
    band = (TILE + BLK, BLK)
    dma = pltpu.SemaphoreType.DMA
    return pl.pallas_call(
        functools.partial(broadcast_multiply, n_row),
        out_shape=jax.ShapeDtypeStruct(block_values.shape, jnp.bfloat16),
        in_specs=[
            pl.BlockSpec(memory_space=pltpu.SMEM),
            pl.BlockSpec(memory_space=pltpu.SMEM),
            pl.BlockSpec(memory_space=pl.ANY),
        ],
        out_specs=pl.BlockSpec(memory_space=pltpu.VMEM),
        scratch_shapes=[
            pltpu.VMEM(block_values.shape, f32),
            pltpu.VMEM((UNITS, GROUPS) + part, f32),
            pltpu.VMEM((5, GROUPS) + part, f32),
            pltpu.VMEM((4, GROUPS) + part[1:], f32),
            pltpu.VMEM((CHUNKS,) + packet, f32),
            pltpu.VMEM((2, CHUNKS) + packet, f32),
            pltpu.VMEM((2, slots) + packet, f32),
            pltpu.VMEM((4,) + held, f32),
            pltpu.VMEM((4,) + held, f32),
            pltpu.VMEM((4,) + band, f32),
            pltpu.VMEM((4,) + band, f32),
            pltpu.VMEM((4,) + band, f32),
            pltpu.VMEM((4,) + band, f32),
            pltpu.VMEM((2, 2 * BLK, 2 * BLK), jnp.bfloat16),
            pltpu.VMEM((2, BLK, 2 * BLK), jnp.bfloat16),
            dma,
            dma((5, GROUPS)), dma((5, GROUPS)),
            dma((4, GROUPS)), dma((4, GROUPS)),
            dma((2, slots)), dma((2, slots)),
            dma((2, GROUPS)), dma((2, GROUPS)),
            dma((2, GROUPS)), dma((2, GROUPS)),
            dma((4, GROUPS)), dma((4, GROUPS)),
            dma((3, SIDE - 1)), dma((3, SIDE)),
        ],
        compiler_params=pltpu.CompilerParams(
            collective_id=0, has_side_effects=True, vmem_limit_bytes=32 * 1024 * 1024
        ),
        cost_estimate=pl.CostEstimate(flops=400_000_000, bytes_accessed=800_000, transcendentals=0),
        name="broadcast_multiply",
    )(section_cols, block_cols, block_values)


def solution(mesh):
    return jax.shard_map(
        functools.partial(shards, mesh.shape["row"]),
        mesh=mesh,
        in_specs=(P("col", "row"), P("col", "row"), P()),
        out_specs=P("col", "row"),
        check_vma=False,
    )
```

time: 601 us -> 81.4 us (0.14)
  waiting for transfers between devices: 518 us -> 0 us
  Pallas kernels: 0 us -> 78.7 us
  blocking collectives: 55.7 us -> 0 us
  between operations: 16.1 us -> 0.01 us
    psum x2 -> x0, waiting for transfers between devices: 517 us -> none  [from_root(): return lax.psum(jnp.where(mine, x, jnp.zeros_like(x)), axis)]
    pallas_call x0 -> x1, Pallas kernels: none -> 78.7 us  [shards(): pl.pallas_call(functools.partial(broadcast_multiply, n_row), out_shape=ja...]
    psum x2 -> x0, blocking collectives: 55.7 us -> none  [from_root(): return lax.psum(jnp.where(mine, x, jnp.zeros_like(x)), axis)]
  transfers between devices with their start and end apart: 2 -> 0, of which waited for: 2 -> 0; matrix products, arithmetic and copies ran while one was open for 1% -> 0% of each run, Pallas kernels for 0% -> 0%
where the time goes in v1:
time: 81.4 us; the launch traced here: 81.2 us
  Pallas kernels  78.7 us (97%)
  local copies, waits for them, and re-layouts  2.49 us (3%)
    pallas_call x1, Pallas kernels, shards(): pl.pallas_call(functools.partial(broadcast_multiply, n_row), out_shape=ja...  78.7 us
    unnamed x6, local copies, waits for them, and re-layouts  2.49 us

profile of v1, /device:TPU:1, one launch (start us, length us, event | category | flops | bytes accessed | tf_op | source)
XLA Modules:
  0.0 81.2 jit_solution(12733457923431701241)
XLA Ops:
  0.0 0.0 copy-start.1
  0.0 0.7 copy.4.cols_ref
  0.7 0.0 copy-done.1
  0.7 0.0 copy-start
  0.8 1.0 %copy-done = f32[1024,128]{1,0:T(8,128)S(1)} copy-done((f32[1024,128]{1,0:T(8,128)S(1)}, f32[1024,128]{1,0:T(8,128)}, u32[]{:S(2)}) %copy-start) | copy-done | bytes 524312
  1.8 78.7 %broadcast_multiply.1 = bf16[1024,128]{1,0:T(8,128)(2,1)S(1)} custom-call(s32[2]{0:T(128)S(1)} %copy-done.1, s32[8,1]{1,0:T(8,128)S(1)} %copy.4.cols_ref, f32[1024,128]{1,0:T(8,128)S(1)} %copy-done), custom_call_target="tpu_custom_call" | custom-call | flops 400000000 | bytes 800000 | tf_op jit(solution)/shard_map/broadcast_multiply/pallas_call | solution.py:319
  80.5 0.7 copy.6
Async XLA Ops:
  0.0 0.7 copy-start.1
  0.7 1.0 %copy-start = (f32[1024,128]{1,0:T(8,128)S(1)}, f32[1024,128]{1,0:T(8,128)}, u32[]{:S(2)}) copy-start(f32[1024,128]{1,0:T(8,128)} %x_hbm.1) | copy-start | bytes 1572868

commit v2 on v1

--- a/solution.py
+++ b/solution.py
@@ -15,7 +15,7 @@
 GROUPS = 3
 PER = 3
 CHUNKS = GROUPS * PER
-LANES = 5
+LANES = 4
 SIDE = 4
 
 
@@ -26,8 +26,9 @@
 ):
     chips = n_row // 2
     blocks = chips // STRIDE
-    hops = (blocks // 2, (blocks - 1) // 2)
-    slots = tuple(CHUNKS + LANES * (d - 1) for d in hops)
+    far_hop = blocks // 2
+    slots = CHUNKS + LANES * (far_hop - 1)
+    whole = slots - LANES
     row = lax.axis_index("row")
     col = lax.axis_index("col")
     z, core = lax.div(row, 2), lax.rem(row, 2)
@@ -158,12 +159,12 @@
                 pan[0, g, h, s, c] = value
 
     def consume(d, t):
-        for hop in range(1, hops[d] + 1):
+        for hop in range(1, far_hop + 1):
             k = t - LANES * (hop - 1)
             if 0 <= k < CHUNKS:
                 g, c = k // PER, k % PER
                 place = hop if d == 0 else blocks - hop
-                for h in range(2):
+                for h in range(2) if hop < far_hop else (d,):
                     for s in range(2):
                         pan[0, g, h, s, c] = jnp.where(
                             where_right[h][s] == place, rx[d, t, h, s], pan[0, g, h, s, c]
@@ -207,15 +208,18 @@
                 wh[s, BLK:, q * BLK : (q + 1) * BLK] = high
                 wl[s, :, q * BLK : (q + 1) * BLK] = low
 
+    def packet(ref, d, t):
+        return ref.at[d, t] if t < whole else ref.at[d, t, d]
+
     def received(d, t):
-        wait_for(rx.at[d, t], cv_r.at[d, t])
+        wait_for(packet(rx, d, t), cv_r.at[d, t])
 
     def finish(t):
-        k = t - LANES * (hops[0] - 1)
+        k = t - LANES * (far_hop - 1)
         if k >= 0 and k % PER == PER - 1:
             gather(k // PER)
 
-    for t in range(slots[0]):
+    for t in range(slots):
         if t < CHUNKS and t % PER == 0:
             g = t // PER
             for i in range(5):
@@ -225,8 +229,6 @@
             for k in range(t, t + PER):
                 candidate(k)
         for d in range(2):
-            if t >= slots[d]:
-                continue
             target = right4 if d == 0 else left4
             if t >= LANES:
                 received(d, t - LANES)
@@ -238,16 +240,14 @@
                             value = jnp.where(where_right[h][s] == 0, value, rx[d, t - LANES, h, s])
                         tx[d, t, h, s] = value
                 source = tx.at[d, t]
+            elif t < whole:
+                source = rx.at[d, t - LANES]
             else:
-                source = rx.at[d, t - LANES]
-            send(source, rx.at[d, t], cv_s.at[d, t], cv_r.at[d, t], target)
+                source = rx.at[d, t - LANES, d]
+            send(source, packet(rx, d, t), cv_s.at[d, t], cv_r.at[d, t], target)
         if t >= LANES:
             for d in range(2):
-                if t < slots[d]:
-                    consume(d, t - LANES)
-            if t >= slots[1] and t - LANES < slots[1]:
-                received(1, t - LANES)
-                consume(1, t - LANES)
+                consume(d, t - LANES)
             finish(t - LANES)
         if t == LANES - 1:
             band_step_two()
@@ -255,12 +255,10 @@
             band_step_three()
         if t == 3 * LANES - 1:
             band_ready()
-    for t in range(slots[0] - LANES, slots[0]):
-        if t < slots[1]:
-            received(1, t)
-            consume(1, t)
-        received(0, t)
-        consume(0, t)
+    for t in range(slots - LANES, slots):
+        for d in range(2):
+            received(d, t)
+            consume(d, t)
         finish(t)
 
     def multiply(buf, i, u):
@@ -289,6 +287,12 @@
     def unit_at(r, i):
         return lax.rem(r + steps[i] + UNITS, UNITS)
 
+    def multiply_sibling(i):
+        for g in range(GROUPS):
+            wait_for(sib.at[i, g], sb_r.at[i, g])
+        multiply(sib, i, unit_at(sibling, i))
+
+    multiply(pan, 0, unit_at(row, 0))
     for i in (1, 2, 3):
         for g in range(GROUPS):
             if i < 3:
@@ -297,12 +301,11 @@
                 wait_for(pan.at[3, g, 0], ah_r.at[0, g])
                 wait_for(pan.at[3, g, 1], ah_r.at[1, g])
             send(pan.at[i, g], sib.at[i, g], sb_s.at[i, g], sb_r.at[i, g], (sibling, col))
-    for i in range(4):
+    multiply_sibling(0)
+    for i in (1, 2, 3):
         multiply(pan, i, unit_at(row, i))
-    for i in range(4):
-        for g in range(GROUPS):
-            wait_for(sib.at[i, g], sb_r.at[i, g])
-        multiply(sib, i, unit_at(sibling, i))
+    for i in (1, 2, 3):
+        multiply_sibling(i)
     for copy in sent:
         copy.wait_send()
 

time: 81.4 us -> 76.7 us (0.942)
  Pallas kernels: 78.7 us -> 73.9 us
    pallas_call x1, Pallas kernels: 78.7 us -> 73.9 us  [shards(): pl.pallas_call(functools.partial(broadcast_multiply, n_row), out_shape=ja...]
where the time goes in v2:
time: 76.7 us; the launch traced here: 76.4 us
  Pallas kernels  73.9 us (96%)
  local copies, waits for them, and re-layouts  2.49 us (3%)
    pallas_call x1, Pallas kernels, shards(): pl.pallas_call(functools.partial(broadcast_multiply, n_row), out_shape=ja...  73.9 us
    unnamed x6, local copies, waits for them, and re-layouts  2.49 us

profile of v2, /device:TPU:1, one launch (start us, length us, event | category | flops | bytes accessed | tf_op | source)
XLA Modules:
  0.0 76.4 jit_solution(15555150315859200243)
XLA Ops:
  0.0 0.0 copy-start.1
  0.0 0.7 copy.4.cols_ref
  0.7 0.0 copy-done.1
  0.7 0.0 copy-start
  0.8 1.0 %copy-done = f32[1024,128]{1,0:T(8,128)S(1)} copy-done((f32[1024,128]{1,0:T(8,128)S(1)}, f32[1024,128]{1,0:T(8,128)}, u32[]{:S(2)}) %copy-start) | copy-done | bytes 524312
  1.8 73.9 %broadcast_multiply.1 = bf16[1024,128]{1,0:T(8,128)(2,1)S(1)} custom-call(s32[2]{0:T(128)S(1)} %copy-done.1, s32[8,1]{1,0:T(8,128)S(1)} %copy.4.cols_ref, f32[1024,128]{1,0:T(8,128)S(1)} %copy-done), custom_call_target="tpu_custom_call" | custom-call | flops 400000000 | bytes 800000 | tf_op jit(solution)/shard_map/broadcast_multiply/pallas_call | solution.py:322
  75.7 0.7 copy.6
Async XLA Ops:
  0.0 0.7 copy-start.1
  0.7 1.0 %copy-start = (f32[1024,128]{1,0:T(8,128)S(1)}, f32[1024,128]{1,0:T(8,128)}, u32[]{:S(2)}) copy-start(f32[1024,128]{1,0:T(8,128)} %x_hbm.1) | copy-start | bytes 1572868

commit v3 on v2

--- a/solution.py
+++ b/solution.py
@@ -20,9 +20,9 @@
 
 
 def broadcast_multiply(
-    n_row, sec_ref, cols_ref, x_hbm, o_ref,
-    xv, xs, raw, rawh, cand, tx, rx, pan, sib, stage, bx, by, bnd, wh, wl,
-    x_sem, rs_s, rs_r, rh_s, rh_r, cv_s, cv_r, ag_s, ag_r, ah_s, ah_r, sb_s, sb_r, bs_s, bs_r,
+    n_row, sec_ref, cols_ref, xv, o_ref,
+    xs, raw, rawh, cand, tx, rx, pan, sib, stage, bx, by, bnd, wh, wl,
+    rs_s, rs_r, rh_s, rh_r, cv_s, cv_r, ag_s, ag_r, ah_s, ah_r, sb_s, sb_r, bs_s, bs_r,
 ):
     chips = n_row // 2
     blocks = chips // STRIDE
@@ -52,10 +52,6 @@
     greet += [(row, cx * SIDE + py) for py in ys_peers]
     for device in greet:
         pl.semaphore_signal(barrier, inc=1, device_id=device, device_id_type=MESH)
-
-    load = pltpu.make_async_copy(x_hbm, xv, x_sem)
-    load.start()
-    load.wait()
 
     sent = []
 
@@ -325,11 +321,10 @@
         in_specs=[
             pl.BlockSpec(memory_space=pltpu.SMEM),
             pl.BlockSpec(memory_space=pltpu.SMEM),
-            pl.BlockSpec(memory_space=pl.ANY),
+            pl.BlockSpec(memory_space=pltpu.VMEM),
         ],
         out_specs=pl.BlockSpec(memory_space=pltpu.VMEM),
         scratch_shapes=[
-            pltpu.VMEM(block_values.shape, f32),
             pltpu.VMEM((UNITS, GROUPS) + part, f32),
             pltpu.VMEM((5, GROUPS) + part, f32),
             pltpu.VMEM((4, GROUPS) + part[1:], f32),
@@ -344,7 +339,6 @@
             pltpu.VMEM((4,) + band, f32),
             pltpu.VMEM((2, 2 * BLK, 2 * BLK), jnp.bfloat16),
             pltpu.VMEM((2, BLK, 2 * BLK), jnp.bfloat16),
-            dma,
             dma((5, GROUPS)), dma((5, GROUPS)),
             dma((4, GROUPS)), dma((4, GROUPS)),
             dma((2, slots)), dma((2, slots)),

time: 76.7 us -> 76.7 us (level)
  no operation moved by 1% of the time
where the time goes in v3:
time: 76.7 us; the launch traced here: 76.4 us
  Pallas kernels  73.9 us (96%)
  local copies, waits for them, and re-layouts  2.49 us (3%)
    pallas_call x1, Pallas kernels, shards(): pl.pallas_call(functools.partial(broadcast_multiply, n_row), out_shape=ja...  73.9 us
    unnamed x6, local copies, waits for them, and re-layouts  2.49 us

profile of v3, /device:TPU:1, one launch (start us, length us, event | category | flops | bytes accessed | tf_op | source)
XLA Modules:
  0.0 76.4 jit_solution(9575578089799473459)
XLA Ops:
  0.0 0.0 copy-start.1
  0.0 0.7 copy.4.cols_ref
  0.7 0.0 copy-done.1
  0.7 0.0 copy-start
  0.8 1.0 %copy-done = f32[1024,128]{1,0:T(8,128)S(1)} copy-done((f32[1024,128]{1,0:T(8,128)S(1)}, f32[1024,128]{1,0:T(8,128)}, u32[]{:S(2)}) %copy-start) | copy-done | bytes 524312
  1.8 73.9 %broadcast_multiply.1 = bf16[1024,128]{1,0:T(8,128)(2,1)S(1)} custom-call(s32[2]{0:T(128)S(1)} %copy-done.1, s32[8,1]{1,0:T(8,128)S(1)} %copy.4.cols_ref, f32[1024,128]{1,0:T(8,128)S(1)} %copy-done), custom_call_target="tpu_custom_call" | custom-call | flops 400000000 | bytes 800000 | tf_op jit(solution)/shard_map/broadcast_multiply/pallas_call | solution.py:318
  75.7 0.7 copy.6
Async XLA Ops:
  0.0 0.7 copy-start.1
  0.7 1.0 %copy-start = (f32[1024,128]{1,0:T(8,128)S(1)}, f32[1024,128]{1,0:T(8,128)}, u32[]{:S(2)}) copy-start(f32[1024,128]{1,0:T(8,128)} %xv.1) | copy-start | bytes 1572868
